TPU v7x, 512 devices: a whole 4x8x8 slice. The times are simulated.
512 devices in a mesh: ia: 8 (over y), ja: 4 (over x), ka: 16 (over z, core).
Axes of the slice: x: 4, y: 8, z: 8, core: 2. Of those that a mesh axis runs over, the one named last changes fastest.
Arguments:
- tensor: bfloat16 [1024, 512, 2048], P('ia', 'ja', 'ka'), may hold values from -6144 to 6144
- factor_b: bfloat16 [64, 4, 128], P(None, 'ja', ('ia', 'ka')), may hold values from -60 to 60
- factor_c: bfloat16 [64, 16, 128], P(None, 'ka', ('ia', 'ja')), may hold values from -60 to 60
Outputs:
- final_a: float32 [64, 8, 128], P(None, 'ia', ('ja', 'ka'))
All inputs are finite; a program needn't handle non-finite values.
Results may differ from a plain program's by a relative error of at most 0.00075.
Values may be sent and summed in bfloat16 or wider, within the bound.
A program may use at most 64 MiB of HBM per device.

v0:
```python
import jax
import jax.numpy as jnp
from jax import lax
from jax.sharding import PartitionSpec as P


def gram_of(rows):
    return jnp.dot(rows, rows.T, preferred_element_type=jnp.float32)


def solve_with(matrix, right_side):
    lower = jnp.linalg.cholesky(matrix)
    return jax.scipy.linalg.cho_solve((lower, True), right_side)


def shards(tensor, factor_b, factor_c):
    slab_b = lax.all_gather(factor_b, ("ia", "ka"), axis=2, tiled=True)[:, 0, :]
    slab_c = lax.all_gather(factor_c, ("ia", "ja"), axis=2, tiled=True)[:, 0, :]
    gram_b, gram_c = lax.psum(
        (gram_of(factor_b[:, 0, :]), gram_of(factor_c[:, 0, :])), ("ia", "ja", "ka")
    )
    inner = lax.dot_general(
        slab_c, tensor, (((1,), (2,)), ((), ())), preferred_element_type=jnp.float32
    )
    partial_a = jnp.sum(inner * slab_b.astype(jnp.float32)[:, None, :], axis=2)
    matrix = gram_b * gram_c
    owned = solve_with(
        matrix, lax.psum_scatter(partial_a, ("ja", "ka"), scatter_dimension=1, tiled=True)
    )
    return owned[:, None, :]


def solution(mesh):
    in_specs = (P("ia", "ja", "ka"), P(None, "ja", ("ia", "ka")), P(None, "ka", ("ia", "ja")))
    out_specs = P(None, "ia", ("ja", "ka"))
    return jax.shard_map(shards, mesh=mesh, in_specs=in_specs, out_specs=out_specs, check_vma=False)
```

profile of v0, /device:TPU:1, one launch (start us, length us, event | category | flops | bytes accessed | tf_op | source)
XLA Modules:
  0.0 458.8 jit_solution(6036455450373540411)
XLA Ops:
  0.0 0.0 copy-start.1
  0.0 0.0 copy-start
  0.0 52.0 %all_gather.7 = bf16[64,1,128]{0,1,2:T(2,128)(2,1)S(1)} all-gather(bf16[64,1,1]{0,1,2:T(2,128)(2,1)} %bitcast.31), channel_id=1, replica_groups=mesh['ia'=8,'ja'=4,'ka'=16] {'ia','ka'}, dimensions={2}, use_global_device_ids=true | all-gather | bytes 16512 | tf_op jit(solution)/shard_map/all_gather | solution.py:17
  52.0 0.1 mul.21
  52.0 0.1 copy.23
  52.1 0.7 copy.20
  52.8 35.9 %all_gather.6 = bf16[64,1,128]{0,1,2:T(2,128)(2,1)S(1)} all-gather(bf16[64,1,4]{0,1,2:T(2,128)(2,1)S(1)} %copy.20), channel_id=1, replica_groups=mesh['ia'=8,'ja'=4,'ka'=16] {'ia','ja'}, dimensions={2}, use_global_device_ids=true | all-gather | bytes 16896 | tf_op jit(solution)/shard_map/all_gather | solution.py:18
  88.7 0.1 copy.21
  88.8 3.9 multiply_reduce_fusion
  92.7 0.1 copy.24
  92.8 253.0 %all-reduce = f32[64,128]{1,0:T(8,128)S(1)} all-reduce(f32[64,128]{1,0:T(8,128)S(1)} %copy.24), channel_id=2, replica_groups=mesh['ia'=8,'ja'=4,'ka'=16] {'ja','ka'}, use_global_device_ids=true, to_apply=%region_5.6.clone | all-reduce | flops 8192 | bytes 65536
  345.7 1.3 dynamic-slice
  347.7 0.0 copy-done.1
  347.7 0.1 broadcast_multiply_fusion
  347.7 0.0 copy-done
  347.7 0.2 fusion.7
  347.9 97.6 %all-reduce.1 = (f32[64,64]{0,1:T(8,128)S(1)}, f32[64,64]{0,1:T(8,128)S(1)}) all-reduce(f32[64,64]{0,1:T(8,128)S(1)} %broadcast_multiply_fusion, f32[64,64]{0,1:T(8,128)S(1)} %fusion.7), channel_id=1, replica_groups=mesh['ia'=8,'ja'=4,'ka'=16] {'ia','ja','ka'}, use_global_device_ids=true, to_apply=%region_0.0 | all-reduce | flops 8192 | bytes 65536 | tf_op jit(solution)/shard_map/psum | solution.py:19
  445.6 0.1 copy.19
  445.7 5.8 %cholesky.16 = f32[64,64]{1,0:T(8,128)S(1)} custom-call(f32[64,64]{1,0:T(8,128)S(1)} %fusion.5), custom_call_target="Cholesky" | custom-call | tf_op jit(solution)/shard_map/jit(cholesky)/cholesky | solution.py:12
  451.6 0.6 compare_reduce_fusion
  452.2 0.7 fusion
  452.9 4.9 %custom-call.10 = f32[1,64,64]{1,2,0:T(8,128)S(1)} custom-call(f32[1,64,64]{2,1,0:T(8,128)S(1)} %fusion), custom_call_target="InvertDiagBlocksLowerTriangular" | custom-call | tf_op jit(solution)/shard_map/jit(_cho_solve)/triangular_solve | solution.py:13
  457.8 0.3 fusion.1
  458.1 0.8 convolution_bitcast_fusion
  (4 shorter events, 0.0 us)
Async XLA Ops:
  0.0 347.7 %copy-start.1 = (bf16[64,1,1]{0,2,1:T(2,128)(2,1)S(1)}, bf16[64,1,1]{0,2,1:T(2,128)(2,1)}, u32[]{:S(2)}) copy-start(bf16[64,1,1]{0,2,1:T(2,128)(2,1)} %param.4) | copy-start | bytes 388
  0.0 347.7 %copy-start = (bf16[64,1,4]{0,2,1:T(4,128)(2,1)S(1)}, bf16[64,1,4]{0,2,1:T(4,128)(2,1)}, u32[]{:S(2)}) copy-start(bf16[64,1,4]{0,2,1:T(4,128)(2,1)} %param.5) | copy-start | bytes 1540
where the time goes:
time: 459 us
  blocking collectives  438 us (95%)
  other arithmetic  12.2 us (3%)
  matrix products  5.11 us (1%)
    unnamed x1, blocking collectives  253 us
    psum x1, blocking collectives, shards(): lax.psum((gram_of(factor_b[:, 0, :]), gram_of(factor_c[:, 0, :])), ('ia',...  97.6 us
    all_gather x1, blocking collectives, shards(): slab_b = lax.all_gather(factor_b, ('ia', 'ka'), axis=2, tiled=True)[:, 0, :]  52 us
    all_gather x1, blocking collectives, shards(): slab_c = lax.all_gather(factor_c, ('ia', 'ja'), axis=2, tiled=True)[:, 0, :]  35.9 us

commit v1 on v0

v1 whole, which is shorter than its diff:
```python
import functools

import jax
import jax.numpy as jnp
from jax import lax
from jax.experimental import pallas as pl
from jax.experimental.pallas import tpu as pltpu
from jax.sharding import PartitionSpec as P

MESH = pl.DeviceIdType.MESH
F32 = jnp.float32
BF16 = jnp.bfloat16
BLOCK = 8


def eliminate(state):
    rank = state.shape[0]
    row_of = lax.broadcasted_iota(jnp.int32, (rank, 128), 0)
    recips = jnp.zeros((rank, 128), F32)
    for first in range(0, rank, BLOCK):
        base = first // 8 * 8
        live = state[base:]
        rows = row_of[base:]
        columns = [jnp.broadcast_to(live[:, first + q : first + q + 1], live.shape) for q in range(BLOCK)]
        marks = recips[base:]
        for q in range(BLOCK):
            at = first + q - base
            recip = 1.0 / columns[q][at : at + 1]
            marks = jnp.where(rows == first + q, recip, marks)
            lower = jnp.where(rows > first + q, columns[q] * recip, 0.0)
            for later in range(q + 1, BLOCK):
                columns[later] = columns[later] - lower * columns[later][at : at + 1]
            live = live - lower * live[at : at + 1]
        state = live if base == 0 else jnp.concatenate([state[:base], live], axis=0)
        recips = marks if base == 0 else jnp.concatenate([recips[:base], marks], axis=0)
    return state, recips


def kernel(
    sizes, tensor_ref, b_ref, c_ref, out_ref,
    tensor, piece, seen, tile_b, tile_c, slab_b, slab_c, gram_b, gram_c, partial, partials,
    load_sem, send_sem, recv_sem,
):
    n_ia, n_ja, n_ka = sizes
    ia, ja, ka = (lax.axis_index(a) for a in ("ia", "ja", "ka"))
    n_own = n_ja * n_ka

    load = pltpu.make_async_copy(tensor_ref, tensor, load_sem)
    load.start()

    def along_y(d):
        return {"ia": lax.rem(ia + d, n_ia)}

    def along_x(d):
        return {"ja": lax.rem(ja + d, n_ja)}

    def along_z(d):
        return {"ka": lax.rem(ka + d, n_ka)}

    barrier = pltpu.get_barrier_semaphore()
    for count, place in ((n_ia, along_y), (n_ja, along_x), (n_ka, along_z)):
        for d in range(1, count):
            pl.semaphore_signal(barrier, inc=1, device_id=place(d), device_id_type=MESH)

    lane = lax.broadcasted_iota(jnp.int32, (128, 128), 1)
    own_c = c_ref[0].astype(F32)
    own_b = b_ref[0].astype(F32)
    piece[0:4, :] = jnp.concatenate([own_c, own_c], axis=1)
    piece[4:5, :] = jnp.concatenate([own_b, own_b], axis=1)
    seen[pl.ds(pl.multiple_of(ia * 8, 8), 8), :] = piece[...]

    pl.semaphore_wait(barrier, n_ia + n_ja + n_ka - 3)

    def send(source, target, stage, place):
        copy = pltpu.make_async_remote_copy(
            src_ref=source, dst_ref=target, send_sem=send_sem.at[stage], recv_sem=recv_sem.at[stage],
            device_id=place, device_id_type=MESH,
        )
        copy.start()

    def wait(buffer, rows, sem):
        part = buffer.at[pl.ds(0, rows)]
        pltpu.make_async_copy(part, part, sem).wait()

    for d in range(1, n_ia):
        send(piece, seen.at[pl.ds(pl.multiple_of(ia * 8, 8), 8)], 0, along_y(d))
    wait(seen, 8 * (n_ia - 1), recv_sem.at[0])

    at_b = pl.ds(pl.multiple_of(ka * 8, 8), 8)
    at_c = pl.ds(pl.multiple_of(ja * 32, 32), 32)
    for q in range(4):
        tile_c[8 * q : 8 * q + 8, :] = seen[pl.ds(q, 8, stride=8), :]
    tile_b[...] = seen[pl.ds(4, 8, stride=8), :]
    for d in range(1, n_ja):
        send(tile_c, slab_c.at[at_c], 1, along_x(d))
    for d in range(1, n_ka):
        send(tile_b, slab_b.at[at_b], 2, along_z(d))
    slab_c[at_c, :] = tile_c[...]
    slab_b[at_b, :] = tile_b[...]
    wait(slab_c, 32 * (n_ja - 1), recv_sem.at[1])

    def packed_gram(slab):
        rows = slab.astype(BF16)
        full = lax.dot_general(rows, rows, (((0,), (0,)), ((), ())), preferred_element_type=F32)
        return jnp.where(lane[:32] < 64, full[0:32], full[32:64])

    at_gram_c = pl.ds(pl.multiple_of(ka * 32, 32), 32)
    at_gram_b = pl.ds(pl.multiple_of(ja * 32, 32), 32)
    gram_c[at_gram_c, :] = packed_gram(slab_c[...])
    for d in range(1, n_ka):
        send(gram_c.at[at_gram_c], gram_c.at[at_gram_c], 3, along_z(d))
    wait(slab_b, 8 * (n_ka - 1), recv_sem.at[2])
    gram_b[at_gram_b, :] = packed_gram(slab_b[...])
    for d in range(1, n_ja):
        send(gram_b.at[at_gram_b], gram_b.at[at_gram_b], 4, along_x(d))

    order_b = jnp.concatenate([slab_b[pl.ds(i, 16, stride=8), :] for i in range(8)], axis=0)
    order_c = jnp.concatenate([slab_c[pl.ds(i, 16, stride=8), :] for i in range(8)], axis=0)
    weights = jnp.concatenate(
        [jnp.where(lane < 64, order_c, 0.0), jnp.where(lane >= 64, order_c, 0.0)], axis=0
    ).astype(BF16)
    load.wait()

    def contract(p, _):
        both = jnp.concatenate([tensor[2 * p], tensor[2 * p + 1]], axis=1)
        inner = jnp.dot(both, weights, preferred_element_type=F32)
        row = jnp.sum(inner * order_b, axis=0, keepdims=True)
        partial[p, 0:1, :] = row
        return 0

    lax.fori_loop(0, n_own, contract, 0, unroll=4)

    me = ja * n_ka + ka

    def hand(d, _):
        owner = lax.rem(me + d, n_own)
        send(
            partial.at[owner, pl.ds(0, 1)], partials.at[me, pl.ds(0, 1)], 5,
            {"ja": lax.div(owner, n_ka), "ka": lax.rem(owner, n_ka)},
        )
        return 0

    lax.fori_loop(1, n_own, hand, 0)
    partials[me, 0:1, :] = partial[me, 0:1, :]

    wait(gram_c, 32 * (n_ka - 1), recv_sem.at[3])
    total_c = gram_c[0:32, :]
    for k in range(1, n_ka):
        total_c = total_c + gram_c[32 * k : 32 * k + 32, :]
    wait(gram_b, 32 * (n_ja - 1), recv_sem.at[4])
    total_b = gram_b[0:32, :]
    for j in range(1, n_ja):
        total_b = total_b + gram_b[32 * j : 32 * j + 32, :]
    matrix = total_b * total_c
    square = jnp.concatenate([matrix, pltpu.roll(matrix, 64, 1)], axis=0)
    row64 = lax.broadcasted_iota(jnp.int32, (64, 128), 0)
    lane64 = lane[:64]
    state = jnp.where(lane64 < 64, square, jnp.where(lane64 - 64 == row64, 1.0, 0.0))
    state, recips = eliminate(state)
    inverse = jnp.where(lane64 < 64, pltpu.roll(state, 64, 1), state)

    part = partials.at[pl.ds(0, n_own - 1), pl.ds(0, 1)]
    pltpu.make_async_copy(part, part, recv_sem.at[5]).wait()
    right = jnp.sum(partials[:, 0, :], axis=0, keepdims=True)
    products = inverse * right
    first = jnp.sum(jnp.where(lane64 < 64, products, 0.0), axis=1, keepdims=True)
    second = jnp.sum(jnp.where(lane64 < 64, 0.0, products), axis=1, keepdims=True)
    middle = jnp.where(lane64 < 64, first, second) * recips
    answer = jnp.sum(inverse * middle, axis=0, keepdims=True)
    out_ref[0, 0:1, :] = answer[:, :64]
    out_ref[0, 1:2, :] = answer[:, 64:]

    wait(seen, 8 * (n_ia - 1), send_sem.at[0])
    wait(slab_c, 32 * (n_ja - 1), send_sem.at[1])
    wait(slab_b, 8 * (n_ka - 1), send_sem.at[2])
    wait(gram_c, 32 * (n_ka - 1), send_sem.at[3])
    wait(gram_b, 32 * (n_ja - 1), send_sem.at[4])
    pltpu.make_async_copy(part, part, send_sem.at[5]).wait()


def shards(sizes, tensor, factor_b, factor_c):
    n_ia, n_ja, n_ka = sizes
    vmem = pl.BlockSpec(memory_space=pltpu.VMEM)
    out = pl.pallas_call(
        functools.partial(kernel, sizes),
        name="als_update",
        out_shape=jax.ShapeDtypeStruct((1, 2, 64), F32),
        in_specs=[pl.BlockSpec(memory_space=pl.ANY), vmem, vmem],
        out_specs=vmem,
        scratch_shapes=[
            pltpu.VMEM((128, 128, 128), BF16),
            pltpu.VMEM((8, 128), F32),
            pltpu.VMEM((8 * n_ia, 128), F32),
            pltpu.VMEM((8, 128), F32),
            pltpu.VMEM((32, 128), F32),
            pltpu.VMEM((8 * n_ka, 128), F32),
            pltpu.VMEM((32 * n_ja, 128), F32),
            pltpu.VMEM((32 * n_ja, 128), F32),
            pltpu.VMEM((32 * n_ka, 128), F32),
            pltpu.VMEM((n_ja * n_ka, 8, 128), F32),
            pltpu.VMEM((n_ja * n_ka, 8, 128), F32),
            pltpu.SemaphoreType.DMA,
            pltpu.SemaphoreType.DMA((6,)),
            pltpu.SemaphoreType.DMA((6,)),
        ],
        compiler_params=pltpu.CompilerParams(
            collective_id=0, has_side_effects=True, vmem_limit_bytes=48 * 1024 * 1024
        ),
    )(tensor, jnp.transpose(factor_b, (1, 2, 0)), jnp.transpose(factor_c, (1, 2, 0)))
    return jnp.transpose(out, (2, 0, 1))


def solution(mesh):
    sizes = tuple(mesh.shape[a] for a in ("ia", "ja", "ka"))
    in_specs = (P("ia", "ja", "ka"), P(None, "ja", ("ia", "ka")), P(None, "ka", ("ia", "ja")))
    out_specs = P(None, "ia", ("ja", "ka"))
    return jax.shard_map(
        functools.partial(shards, sizes), mesh=mesh, in_specs=in_specs, out_specs=out_specs, check_vma=False
    )
```

time: 459 us -> 39.8 us (0.09)
  blocking collectives: 438 us -> 0 us
  Pallas kernels: 0 us -> 35.5 us
  other arithmetic: 12.2 us -> 0 us
  matrix products: 5.11 us -> 0 us
    unnamed x1 -> x0, blocking collectives: 253 us -> none
    psum x1 -> x0, blocking collectives: 97.6 us -> none  [shards(): lax.psum((gram_of(factor_b[:, 0, :]), gram_of(factor_c[:, 0, :])), ('ia',...]
    all_gather x2 -> x0, blocking collectives: 87.9 us -> none  [the longest x1 52 us: shards(): slab_b = lax.all_gather(factor_b, ('ia', 'ka'), axis=2, tiled=True)[:, 0, :]]
    pallas_call x0 -> x1, Pallas kernels: none -> 35.5 us  [shards(): pl.pallas_call(functools.partial(kernel, sizes), name='als_update', out_s...]
    another operation x6 -> x0, other arithmetic: 12.1 us -> none  [the longest x3 6.52 us: solve_with(): lower = jnp.linalg.cholesky(matrix)]
where the time goes in v1:
time: 39.8 us; the launch traced here: 39.6 us
  Pallas kernels  35.5 us (89%)
  local copies, waits for them, and re-layouts  4.09 us (10%)
    pallas_call x1, Pallas kernels, shards(): pl.pallas_call(functools.partial(kernel, sizes), name='als_update', out_s...  35.5 us
    unnamed x7, local copies, waits for them, and re-layouts  4.09 us

profile of v1, /device:TPU:1, one launch (start us, length us, event | category | flops | bytes accessed | tf_op | source)
XLA Modules:
  0.0 39.6 jit_solution(2496457948843464495)
XLA Ops:
  0.0 0.0 copy-start
  0.0 2.2 %copy-done = bf16[128,128,128]{2,1,0:T(8,128)(2,1)S(1)} copy-done((bf16[128,128,128]{2,1,0:T(8,128)(2,1)S(1)}, bf16[128,128,128]{2,1,0:T(8,128)(2,1)}, u32[]{:S(2)}) %copy-start) | copy-done | bytes 4194328
  2.2 0.0 copy-start.1
  2.2 0.7 %copy-done.1 = bf16[64,1,4]{0,2,1:T(4,128)(2,1)S(1)} copy-done((bf16[64,1,4]{0,2,1:T(4,128)(2,1)S(1)}, bf16[64,1,4]{0,2,1:T(4,128)(2,1)}, u32[]{:S(2)}) %copy-start.1) | copy-done | bytes 536
  2.9 0.0 copy-start.2
  2.9 0.7 %copy-done.2 = bf16[64,1,1]{0,2,1:T(2,128)(2,1)S(1)} copy-done((bf16[64,1,1]{0,2,1:T(2,128)(2,1)S(1)}, bf16[64,1,1]{0,2,1:T(2,128)(2,1)}, u32[]{:S(2)}) %copy-start.2) | copy-done | bytes 152
  3.5 35.5 %als_update.1 = f32[1,2,64]{2,1,0:T(2,128)S(1)} custom-call(bf16[128,128,128]{2,1,0:T(8,128)(2,1)S(1)} %copy-done, bf16[1,1,64]{2,1,0:T(2,128)(2,1)S(1)} %bitcast.5, bf16[1,4,64]{2,1,0:T(4,128)(2,1)S(1)} %bitcast.4), custom_call_target="tpu_custom_call" | custom-call | tf_op jit(solution)/shard_map/als_update/pallas_call | solution.py:184
  39.0 0.6 %copy.5 = f32[64,1,2]{0,2,1:T(2,128)} copy(f32[64,1,2]{0,2,1:T(2,128)S(1)} %bitcast.3) | data formatting | bytes 1024
Async XLA Ops:
  0.0 2.2 %copy-start = (bf16[128,128,128]{2,1,0:T(8,128)(2,1)S(1)}, bf16[128,128,128]{2,1,0:T(8,128)(2,1)}, u32[]{:S(2)}) copy-start(bf16[128,128,128]{2,1,0:T(8,128)(2,1)} %tensor_ref.1) | copy-start | bytes 12582916
  2.2 0.7 %copy-start.1 = (bf16[64,1,4]{0,2,1:T(4,128)(2,1)S(1)}, bf16[64,1,4]{0,2,1:T(4,128)(2,1)}, u32[]{:S(2)}) copy-start(bf16[64,1,4]{0,2,1:T(4,128)(2,1)} %param.5) | copy-start | bytes 1540
  2.9 0.7 %copy-start.2 = (bf16[64,1,1]{0,2,1:T(2,128)(2,1)S(1)}, bf16[64,1,1]{0,2,1:T(2,128)(2,1)}, u32[]{:S(2)}) copy-start(bf16[64,1,1]{0,2,1:T(2,128)(2,1)} %param.4) | copy-start | bytes 388

commit v2 on v1

v2 whole, which is shorter than its diff:
```python
import functools

import jax
import jax.numpy as jnp
from jax import lax
from jax.experimental import pallas as pl
from jax.experimental.pallas import tpu as pltpu
from jax.sharding import PartitionSpec as P

MESH = pl.DeviceIdType.MESH
F32 = jnp.float32
BF16 = jnp.bfloat16
BLOCK = 8


def eliminate(state):
    rank = state.shape[0]
    row_of = lax.broadcasted_iota(jnp.int32, (rank, 128), 0)
    recips = jnp.zeros((rank, 128), F32)
    for first in range(0, rank, BLOCK):
        base = first // 8 * 8
        live = state[base:]
        rows = row_of[base:]
        columns = [jnp.broadcast_to(live[:, first + q : first + q + 1], live.shape) for q in range(BLOCK)]
        marks = recips[base:]
        for q in range(BLOCK):
            at = first + q - base
            recip = 1.0 / columns[q][at : at + 1]
            marks = jnp.where(rows == first + q, recip, marks)
            lower = jnp.where(rows > first + q, columns[q] * recip, 0.0)
            for later in range(q + 1, BLOCK):
                columns[later] = columns[later] - lower * columns[later][at : at + 1]
            live = live - lower * live[at : at + 1]
        state = live if base == 0 else jnp.concatenate([state[:base], live], axis=0)
        recips = marks if base == 0 else jnp.concatenate([recips[:base], marks], axis=0)
    return state, recips


def far_first(count):
    return sorted(range(1, count), key=lambda d: -min(d, count - d))


def kernel(
    sizes, tensor_ref, b_ref, c_ref, out_ref,
    tensor, own_b, own_c, piece, seen, tile_b, tile_c, slab_b, slab_c, wide_c, gram_b, gram_c, matrix, partial, partials,
    load_sem, ready, send_sem, recv_sem,
):
    n_ia, n_ja, n_ka = sizes
    n_z = n_ka // 2
    ia, ja, ka = (lax.axis_index(a) for a in ("ia", "ja", "ka"))
    z, core = lax.div(ka, 2), lax.rem(ka, 2)
    n_own = n_ja * n_ka

    load_c = pltpu.make_async_copy(c_ref, own_c, load_sem.at[0])
    load_b = pltpu.make_async_copy(b_ref, own_b, load_sem.at[1])
    load = pltpu.make_async_copy(tensor_ref, tensor, load_sem.at[2])
    load_c.start()
    load_b.start()

    def along_y(d):
        return {"ia": lax.rem(ia + d, n_ia)}

    def along_x(dx, dc):
        return {"ja": lax.rem(ja + dx, n_ja), "ka": 2 * z + lax.rem(core + dc, 2)}

    def along_z(d):
        return {"ka": 2 * lax.rem(z + d, n_z) + core}

    ys = far_first(n_ia)
    zs = far_first(n_z)
    xs = [(dx, dc) for dx in far_first(n_ja) + [0] for dc in (0, 1) if dx or dc]

    barrier = pltpu.get_barrier_semaphore()

    def signal(sem, place):
        pl.semaphore_signal(sem, inc=1, device_id=place, device_id_type=MESH)

    for d in ys:
        signal(barrier, along_y(d))
    for dx, dc in xs:
        signal(barrier, along_x(dx, dc))

    def greet_higher(k, _):
        signal(barrier, {"ka": k})
        return 0

    lax.fori_loop(2 * z + 2, n_ka, greet_higher, 0)
    load.start()

    load_c.wait()
    load_b.wait()
    lane = lax.broadcasted_iota(jnp.int32, (128, 128), 1)
    c_rows = own_c[0].astype(F32)
    b_row = own_b[0].astype(F32)
    piece[0:4, :] = jnp.concatenate([c_rows, c_rows], axis=1)
    piece[4:5, :] = jnp.concatenate([b_row, b_row], axis=1)
    seen[pl.ds(pl.multiple_of(ia * 8, 8), 8), :] = piece[...]

    pl.semaphore_wait(barrier, n_ia - 1 + 2 * n_ja - 1 + 2 * z)

    def greet_lower(k, _):
        signal(ready, {"ka": k})
        return 0

    sent = []

    def send(source, target, stage, place):
        pltpu.make_async_remote_copy(
            src_ref=source, dst_ref=target, send_sem=send_sem.at[stage], recv_sem=recv_sem.at[stage],
            device_id=place, device_id_type=MESH,
        ).start()

    def wait(part, sem):
        pltpu.make_async_copy(part, part, sem).wait()

    for d in ys:
        send(piece, seen.at[pl.ds(pl.multiple_of(ia * 8, 8), 8)], 0, along_y(d))
    lax.fori_loop(0, 2 * z, greet_lower, 0)
    part = seen.at[pl.ds(0, 8 * (n_ia - 1))]
    sent.append((part, 0))
    wait(part, recv_sem.at[0])

    at_b = pl.ds(pl.multiple_of(ka * 8, 8), 8)
    at_c = pl.ds(pl.multiple_of((core * n_ja + ja) * 32, 32), 32)
    tile_c[...] = jnp.concatenate([seen[pl.ds(q, 8, stride=8), :] for q in range(4)], axis=0).astype(BF16)
    tile_b[...] = seen[pl.ds(4, 8, stride=8), :]
    for dx, dc in xs:
        send(tile_c, slab_c.at[at_c], 1, along_x(dx, dc))

    def send_b(k, _):
        send(tile_b, slab_b.at[at_b], 2, {"ka": k})
        return 0

    lax.fori_loop(0, 2 * z, send_b, 0)
    send_b(2 * z + 1 - core, 0)

    @pl.when(z < n_z - 1)
    def _():
        pl.semaphore_wait(ready, n_ka - 2 - 2 * z)

    lax.fori_loop(2 * z + 2, n_ka, send_b, 0)
    slab_c[at_c, :] = tile_c[...]
    slab_b[at_b, :] = tile_b[...]
    part = slab_c.at[pl.ds(0, 32 * (2 * n_ja - 1))]
    sent.append((part, 1))
    wait(part, recv_sem.at[1])

    def packed_gram(rows):
        full = lax.dot_general(rows, rows, (((0,), (0,)), ((), ())), preferred_element_type=F32)
        both = jnp.where(lane[:32] < 64, full[0:32], full[32:64])
        return jnp.where(core == 0, both[0:16], both[16:32])

    at_gram_c = pl.ds(pl.multiple_of(z * 16, 16), 16)
    at_gram_b = pl.ds(pl.multiple_of(ja * 16, 16), 16)
    gram_c[at_gram_c, :] = packed_gram(slab_c[...])
    for d in zs:
        send(gram_c.at[at_gram_c], gram_c.at[at_gram_c], 3, along_z(d))
    part_c = gram_c.at[pl.ds(0, 16 * (n_z - 1))]
    wide_c[...] = slab_c[pl.ds(pl.multiple_of(core * n_ja * 32, 32), n_ja * 32), :].astype(F32)
    order_c = jnp.concatenate([wide_c[pl.ds(i, 16, stride=8), :] for i in range(8)], axis=0)
    weights = jnp.concatenate(
        [jnp.where(lane < 64, order_c, 0.0), jnp.where(lane >= 64, order_c, 0.0)], axis=0
    ).astype(BF16)
    load.wait()
    part = slab_b.at[pl.ds(0, 8 * (n_ka - 1))]
    sent.append((part, 2))
    wait(part, recv_sem.at[2])
    order_b = jnp.concatenate([slab_b[pl.ds(i, 16, stride=8), :] for i in range(8)], axis=0)

    me = ja * n_ka + ka

    def contract(step, _):
        dz = n_z // 2 + lax.div(step + 1, 2) * (1 - 2 * lax.rem(step, 2))
        owners = [
            (dx, dc, lax.rem(ja + dx, n_ja), 2 * lax.rem(z + dz, n_z) + lax.rem(core + dc, 2))
            for dx in far_first(n_ja) + [0]
            for dc in (1, 0)
        ]
        for dx, dc, x, k in owners:
            p = x * n_ka + k
            both = jnp.concatenate([tensor[2 * p], tensor[2 * p + 1]], axis=1)
            inner = jnp.dot(both, weights, preferred_element_type=F32)
            partial[p, 0:1, :] = jnp.sum(inner * order_b, axis=0, keepdims=True)
        for dx, dc, x, k in owners:
            p = x * n_ka + k

            def hand(x=x, k=k, p=p):
                send(partial.at[p, pl.ds(0, 1)], partials.at[me, pl.ds(0, 1)], 5, {"ja": x, "ka": k})

            if dx or dc:
                hand()
            else:
                pl.when(step < n_z - 1)(hand)
        return 0

    lax.fori_loop(0, n_z, contract, 0)
    partials[me, 0:1, :] = partial[me, 0:1, :]
    part_r = partials.at[pl.ds(0, n_own - 1), pl.ds(0, 1)]

    gram_b[at_gram_b, :] = packed_gram(slab_b[...].astype(BF16))
    for d in far_first(n_ja):
        send(gram_b.at[at_gram_b], gram_b.at[at_gram_b], 4, along_x(d, 0))
    part_b = gram_b.at[pl.ds(0, 16 * (n_ja - 1))]
    sent += [(part_c, 3), (part_b, 4), (part_r, 5)]

    wait(part_c, recv_sem.at[3])
    total_c = gram_c[0:16, :]
    for k in range(1, n_z):
        total_c = total_c + gram_c[16 * k : 16 * k + 16, :]
    wait(part_b, recv_sem.at[4])
    total_b = gram_b[0:16, :]
    for j in range(1, n_ja):
        total_b = total_b + gram_b[16 * j : 16 * j + 16, :]
    at_half = pl.ds(pl.multiple_of(core * 16, 16), 16)
    matrix[at_half, :] = total_b * total_c
    send(matrix.at[at_half], matrix.at[at_half], 6, along_x(0, 1))
    part = matrix.at[pl.ds(0, 16)]
    sent.append((part, 6))
    wait(part, recv_sem.at[6])
    packed = matrix[...]
    square = jnp.concatenate([packed, pltpu.roll(packed, 64, 1)], axis=0)
    row64 = lax.broadcasted_iota(jnp.int32, (64, 128), 0)
    lane64 = lane[:64]
    state = jnp.where(lane64 < 64, square, jnp.where(lane64 - 64 == row64, 1.0, 0.0))
    state, recips = eliminate(state)
    inverse = jnp.where(lane64 < 64, pltpu.roll(state, 64, 1), state)

    wait(part_r, recv_sem.at[5])
    right = jnp.sum(partials[:, 0, :], axis=0, keepdims=True)
    products = inverse * right
    first = jnp.sum(jnp.where(lane64 < 64, products, 0.0), axis=1, keepdims=True)
    second = jnp.sum(jnp.where(lane64 < 64, 0.0, products), axis=1, keepdims=True)
    middle = jnp.where(lane64 < 64, first, second) * recips
    answer = jnp.sum(inverse * middle, axis=0, keepdims=True)
    out_ref[0, 0:1, :] = answer[:, :64]
    out_ref[0, 1:2, :] = answer[:, 64:]

    for part, stage in sent:
        wait(part, send_sem.at[stage])


def shards(sizes, tensor, factor_b, factor_c):
    n_ia, n_ja, n_ka = sizes
    arrays = (tensor, jnp.transpose(factor_b, (1, 2, 0)), jnp.transpose(factor_c, (1, 2, 0)))
    in_hbm = pl.BlockSpec(memory_space=pltpu.HBM)
    out = pl.pallas_call(
        functools.partial(kernel, sizes),
        name="als_update",
        out_shape=jax.ShapeDtypeStruct((1, 2, 64), F32),
        in_specs=[in_hbm, in_hbm, in_hbm],
        out_specs=pl.BlockSpec(memory_space=pltpu.VMEM),
        scratch_shapes=[
            pltpu.VMEM((128, 128, 128), BF16),
            pltpu.VMEM((1, 1, 64), BF16),
            pltpu.VMEM((1, 4, 64), BF16),
            pltpu.VMEM((8, 128), F32),
            pltpu.VMEM((8 * n_ia, 128), F32),
            pltpu.VMEM((8, 128), F32),
            pltpu.VMEM((32, 128), BF16),
            pltpu.VMEM((8 * n_ka, 128), F32),
            pltpu.VMEM((2 * 32 * n_ja, 128), BF16),
            pltpu.VMEM((32 * n_ja, 128), F32),
            pltpu.VMEM((16 * n_ja, 128), F32),
            pltpu.VMEM((16 * n_ka // 2, 128), F32),
            pltpu.VMEM((32, 128), F32),
            pltpu.VMEM((n_ja * n_ka, 8, 128), F32),
            pltpu.VMEM((n_ja * n_ka, 8, 128), F32),
            pltpu.SemaphoreType.DMA((3,)),
            pltpu.SemaphoreType.REGULAR,
            pltpu.SemaphoreType.DMA((7,)),
            pltpu.SemaphoreType.DMA((7,)),
        ],
        compiler_params=pltpu.CompilerParams(
            collective_id=0, has_side_effects=True, vmem_limit_bytes=48 * 1024 * 1024
        ),
    )(*(pltpu.with_memory_space_constraint(array, pltpu.HBM) for array in arrays))
    return jnp.transpose(out, (2, 0, 1))


def solution(mesh):
    sizes = tuple(mesh.shape[a] for a in ("ia", "ja", "ka"))
    in_specs = (P("ia", "ja", "ka"), P(None, "ja", ("ia", "ka")), P(None, "ka", ("ia", "ja")))
    out_specs = P(None, "ia", ("ja", "ka"))
    return jax.shard_map(
        functools.partial(shards, sizes), mesh=mesh, in_specs=in_specs, out_specs=out_specs, check_vma=False
    )
```

time: 39.8 us -> 32.9 us (0.83)
  local copies, waits for them, and re-layouts: 4.09 us -> 0.56 us
  Pallas kernels: 35.5 us -> 32.2 us
    unnamed x7 -> x1, local copies, waits for them, and re-layouts: 4.09 us -> 0.56 us
    pallas_call x1, Pallas kernels: 35.5 us -> 32.2 us  [shards(): pl.pallas_call(functools.partial(kernel, sizes), name='als_update', out_s...]
where the time goes in v2:
time: 32.9 us; the launch traced here: 32.8 us
  Pallas kernels  32.2 us (98%)
  local copies, waits for them, and re-layouts  0.56 us (2%)
    pallas_call x1, Pallas kernels, shards(): pl.pallas_call(functools.partial(kernel, sizes), name='als_update', out_s...  32.2 us

profile of v2, /device:TPU:1, one launch (start us, length us, event | category | flops | bytes accessed | tf_op | source)
XLA Modules:
  0.0 32.8 jit_solution(9412098601825815209)
XLA Ops:
  0.0 32.2 %als_update.1 = f32[1,2,64]{2,1,0:T(2,128)S(1)} custom-call(bf16[128,128,128]{2,1,0:T(8,128)(2,1)} %tensor_ref.1, bf16[1,1,64]{2,1,0:T(2,128)(2,1)} %bitcast.5, bf16[1,4,64]{2,1,0:T(4,128)(2,1)} %bitcast.4), custom_call_target="tpu_custom_call" | custom-call | tf_op jit(solution)/shard_map/als_update/pallas_call | solution.py:246
  32.2 0.6 %copy.5 = f32[64,1,2]{0,2,1:T(2,128)} copy(f32[64,1,2]{0,2,1:T(2,128)S(1)} %bitcast.3) | data formatting | bytes 1024

commit v3 on v2

--- a/solution.py
+++ b/solution.py
@@ -10,7 +10,7 @@
 MESH = pl.DeviceIdType.MESH
 F32 = jnp.float32
 BF16 = jnp.bfloat16
-BLOCK = 8
+BLOCK = 16
 
 
 def eliminate(state):
@@ -42,7 +42,7 @@
 
 def kernel(
     sizes, tensor_ref, b_ref, c_ref, out_ref,
-    tensor, own_b, own_c, piece, seen, tile_b, tile_c, slab_b, slab_c, wide_c, gram_b, gram_c, matrix, partial, partials,
+    tensor, own_b, own_c, piece, seen, tile_b, tile_c, slab_b, slab_c, wide_c, gram_b, gram_c, matrix, inner, partial, partials,
     load_sem, ready, send_sem, recv_sem,
 ):
     n_ia, n_ja, n_ka = sizes
@@ -50,6 +50,7 @@
     ia, ja, ka = (lax.axis_index(a) for a in ("ia", "ja", "ka"))
     z, core = lax.div(ka, 2), lax.rem(ka, 2)
     n_own = n_ja * n_ka
+    half = n_z // 2
 
     load_c = pltpu.make_async_copy(c_ref, own_c, load_sem.at[0])
     load_b = pltpu.make_async_copy(b_ref, own_b, load_sem.at[1])
@@ -63,11 +64,7 @@
     def along_x(dx, dc):
         return {"ja": lax.rem(ja + dx, n_ja), "ka": 2 * z + lax.rem(core + dc, 2)}
 
-    def along_z(d):
-        return {"ka": 2 * lax.rem(z + d, n_z) + core}
-
     ys = far_first(n_ia)
-    zs = far_first(n_z)
     xs = [(dx, dc) for dx in far_first(n_ja) + [0] for dc in (0, 1) if dx or dc]
 
     barrier = pltpu.get_barrier_semaphore()
@@ -77,8 +74,14 @@
 
     for d in ys:
         signal(barrier, along_y(d))
-    for dx, dc in xs:
-        signal(barrier, along_x(dx, dc))
+    signal(barrier, along_x(0, 1))
+
+    def greet_higher_x(x, _):
+        for c in (0, 1):
+            signal(barrier, {"ja": x, "ka": 2 * z + c})
+        return 0
+
+    lax.fori_loop(ja + 1, n_ja, greet_higher_x, 0)
 
     def greet_higher(k, _):
         signal(barrier, {"ka": k})
@@ -96,10 +99,15 @@
     piece[4:5, :] = jnp.concatenate([b_row, b_row], axis=1)
     seen[pl.ds(pl.multiple_of(ia * 8, 8), 8), :] = piece[...]
 
-    pl.semaphore_wait(barrier, n_ia - 1 + 2 * n_ja - 1 + 2 * z)
+    pl.semaphore_wait(barrier, n_ia + 2 * ja + 2 * z)
 
     def greet_lower(k, _):
-        signal(ready, {"ka": k})
+        signal(ready.at[0], {"ka": k})
+        return 0
+
+    def greet_lower_x(x, _):
+        for c in (0, 1):
+            signal(ready.at[1], {"ja": x, "ka": 2 * z + c})
         return 0
 
     sent = []
@@ -116,9 +124,15 @@
     for d in ys:
         send(piece, seen.at[pl.ds(pl.multiple_of(ia * 8, 8), 8)], 0, along_y(d))
     lax.fori_loop(0, 2 * z, greet_lower, 0)
+    lax.fori_loop(0, ja, greet_lower_x, 0)
     part = seen.at[pl.ds(0, 8 * (n_ia - 1))]
     sent.append((part, 0))
     wait(part, recv_sem.at[0])
+
+    @pl.when(ja < n_ja - 1)
+    def _():
+        pl.semaphore_wait(ready.at[1], 2 * (n_ja - 1 - ja))
+
 
     at_b = pl.ds(pl.multiple_of(ka * 8, 8), 8)
     at_c = pl.ds(pl.multiple_of((core * n_ja + ja) * 32, 32), 32)
@@ -136,7 +150,7 @@
 
     @pl.when(z < n_z - 1)
     def _():
-        pl.semaphore_wait(ready, n_ka - 2 - 2 * z)
+        pl.semaphore_wait(ready.at[0], n_ka - 2 - 2 * z)
 
     lax.fori_loop(2 * z + 2, n_ka, send_b, 0)
     slab_c[at_c, :] = tile_c[...]
@@ -153,8 +167,15 @@
     at_gram_c = pl.ds(pl.multiple_of(z * 16, 16), 16)
     at_gram_b = pl.ds(pl.multiple_of(ja * 16, 16), 16)
     gram_c[at_gram_c, :] = packed_gram(slab_c[...])
-    for d in zs:
-        send(gram_c.at[at_gram_c], gram_c.at[at_gram_c], 3, along_z(d))
+
+    def send_gram(to_z, _):
+        @pl.when(to_z != z)
+        def _():
+            send(gram_c.at[at_gram_c], gram_c.at[at_gram_c], 3, {"ka": 2 * to_z + core})
+
+        return 0
+
+    lax.fori_loop(0, n_z, send_gram, 0)
     part_c = gram_c.at[pl.ds(0, 16 * (n_z - 1))]
     wide_c[...] = slab_c[pl.ds(pl.multiple_of(core * n_ja * 32, 32), n_ja * 32), :].astype(F32)
     order_c = jnp.concatenate([wide_c[pl.ds(i, 16, stride=8), :] for i in range(8)], axis=0)
@@ -162,25 +183,40 @@
         [jnp.where(lane < 64, order_c, 0.0), jnp.where(lane >= 64, order_c, 0.0)], axis=0
     ).astype(BF16)
     load.wait()
+
+    def product(p):
+        both = jnp.concatenate([tensor[2 * p], tensor[2 * p + 1]], axis=1)
+        return jnp.dot(both, weights, preferred_element_type=F32)
+
+    def contract(p, _):
+        inner[p] = product(p)
+        return 0
+
+    @pl.when(z < half)
+    def _():
+        lax.fori_loop(0, n_own, contract, 0, unroll=4)
+
     part = slab_b.at[pl.ds(0, 8 * (n_ka - 1))]
     sent.append((part, 2))
     wait(part, recv_sem.at[2])
+
+    gram_b[at_gram_b, :] = packed_gram(slab_b[...].astype(BF16))
+    for d in far_first(n_ja):
+        send(gram_b.at[at_gram_b], gram_b.at[at_gram_b], 4, along_x(d, 0))
+    part_b = gram_b.at[pl.ds(0, 16 * (n_ja - 1))]
+
     order_b = jnp.concatenate([slab_b[pl.ds(i, 16, stride=8), :] for i in range(8)], axis=0)
-
     me = ja * n_ka + ka
 
-    def contract(step, _):
-        dz = n_z // 2 + lax.div(step + 1, 2) * (1 - 2 * lax.rem(step, 2))
+    def weigh(made, to_z, _):
         owners = [
-            (dx, dc, lax.rem(ja + dx, n_ja), 2 * lax.rem(z + dz, n_z) + lax.rem(core + dc, 2))
+            (dx, dc, lax.rem(ja + dx, n_ja), 2 * to_z + lax.rem(core + dc, 2))
             for dx in far_first(n_ja) + [0]
             for dc in (1, 0)
         ]
         for dx, dc, x, k in owners:
             p = x * n_ka + k
-            both = jnp.concatenate([tensor[2 * p], tensor[2 * p + 1]], axis=1)
-            inner = jnp.dot(both, weights, preferred_element_type=F32)
-            partial[p, 0:1, :] = jnp.sum(inner * order_b, axis=0, keepdims=True)
+            partial[p, 0:1, :] = jnp.sum(made(p) * order_b, axis=0, keepdims=True)
         for dx, dc, x, k in owners:
             p = x * n_ka + k
 
@@ -190,17 +226,19 @@
             if dx or dc:
                 hand()
             else:
-                pl.when(step < n_z - 1)(hand)
-        return 0
-
-    lax.fori_loop(0, n_z, contract, 0)
+                pl.when(to_z != z)(hand)
+        return 0
+
+    @pl.when(z < half)
+    def _():
+        lax.fori_loop(0, n_z, functools.partial(weigh, lambda p: inner[p]), 0)
+
+    @pl.when(z >= half)
+    def _():
+        lax.fori_loop(0, n_z, functools.partial(weigh, product), 0)
+
     partials[me, 0:1, :] = partial[me, 0:1, :]
     part_r = partials.at[pl.ds(0, n_own - 1), pl.ds(0, 1)]
-
-    gram_b[at_gram_b, :] = packed_gram(slab_b[...].astype(BF16))
-    for d in far_first(n_ja):
-        send(gram_b.at[at_gram_b], gram_b.at[at_gram_b], 4, along_x(d, 0))
-    part_b = gram_b.at[pl.ds(0, 16 * (n_ja - 1))]
     sent += [(part_c, 3), (part_b, 4), (part_r, 5)]
 
     wait(part_c, recv_sem.at[3])
@@ -263,10 +301,11 @@
             pltpu.VMEM((16 * n_ja, 128), F32),
             pltpu.VMEM((16 * n_ka // 2, 128), F32),
             pltpu.VMEM((32, 128), F32),
+            pltpu.VMEM((n_ja * n_ka, 128, 128), F32),
             pltpu.VMEM((n_ja * n_ka, 8, 128), F32),
             pltpu.VMEM((n_ja * n_ka, 8, 128), F32),
             pltpu.SemaphoreType.DMA((3,)),
-            pltpu.SemaphoreType.REGULAR,
+            pltpu.SemaphoreType.REGULAR((2,)),
             pltpu.SemaphoreType.DMA((7,)),
             pltpu.SemaphoreType.DMA((7,)),
         ],

time: 32.9 us -> 31 us (0.942)
  Pallas kernels: 32.2 us -> 30.3 us
    pallas_call x1, Pallas kernels: 32.2 us -> 30.3 us  [shards(): pl.pallas_call(functools.partial(kernel, sizes), name='als_update', out_s...]
where the time goes in v3:
time: 31 us; the launch traced here: 30.9 us
  Pallas kernels  30.3 us (98%)
  local copies, waits for them, and re-layouts  0.56 us (2%)
    pallas_call x1, Pallas kernels, shards(): pl.pallas_call(functools.partial(kernel, sizes), name='als_update', out_s...  30.3 us

profile of v3, /device:TPU:1, one launch (start us, length us, event | category | flops | bytes accessed | tf_op | source)
XLA Modules:
  0.0 30.9 jit_solution(6178223657478961747)
XLA Ops:
  0.0 30.3 %als_update.1 = f32[1,2,64]{2,1,0:T(2,128)S(1)} custom-call(bf16[128,128,128]{2,1,0:T(8,128)(2,1)} %tensor_ref.1, bf16[1,1,64]{2,1,0:T(2,128)(2,1)} %bitcast.5, bf16[1,4,64]{2,1,0:T(4,128)(2,1)} %bitcast.4), custom_call_target="tpu_custom_call" | custom-call | tf_op jit(solution)/shard_map/als_update/pallas_call | solution.py:284
  30.3 0.6 %copy.5 = f32[64,1,2]{0,2,1:T(2,128)} copy(f32[64,1,2]{0,2,1:T(2,128)S(1)} %bitcast.3) | data formatting | bytes 1024

commit v4 on v3

--- a/solution.py
+++ b/solution.py
@@ -167,21 +167,21 @@
     at_gram_c = pl.ds(pl.multiple_of(z * 16, 16), 16)
     at_gram_b = pl.ds(pl.multiple_of(ja * 16, 16), 16)
     gram_c[at_gram_c, :] = packed_gram(slab_c[...])
-
-    def send_gram(to_z, _):
-        @pl.when(to_z != z)
-        def _():
-            send(gram_c.at[at_gram_c], gram_c.at[at_gram_c], 3, {"ka": 2 * to_z + core})
-
-        return 0
-
-    lax.fori_loop(0, n_z, send_gram, 0)
-    part_c = gram_c.at[pl.ds(0, 16 * (n_z - 1))]
     wide_c[...] = slab_c[pl.ds(pl.multiple_of(core * n_ja * 32, 32), n_ja * 32), :].astype(F32)
     order_c = jnp.concatenate([wide_c[pl.ds(i, 16, stride=8), :] for i in range(8)], axis=0)
     weights = jnp.concatenate(
         [jnp.where(lane < 64, order_c, 0.0), jnp.where(lane >= 64, order_c, 0.0)], axis=0
     ).astype(BF16)
+
+    def send_gram(to_z, _):
+        @pl.when(to_z != z)
+        def _():
+            send(gram_c.at[at_gram_c], gram_c.at[at_gram_c], 3, {"ka": 2 * to_z + core})
+
+        return 0
+
+    lax.fori_loop(0, n_z, send_gram, 0)
+    part_c = gram_c.at[pl.ds(0, 16 * (n_z - 1))]
     load.wait()
 
     def product(p):
@@ -200,9 +200,11 @@
     sent.append((part, 2))
     wait(part, recv_sem.at[2])
 
-    gram_b[at_gram_b, :] = packed_gram(slab_b[...].astype(BF16))
-    for d in far_first(n_ja):
-        send(gram_b.at[at_gram_b], gram_b.at[at_gram_b], 4, along_x(d, 0))
+    def share_gram_b():
+        gram_b[at_gram_b, :] = packed_gram(slab_b[...].astype(BF16))
+        for d in far_first(n_ja):
+            send(gram_b.at[at_gram_b], gram_b.at[at_gram_b], 4, along_x(d, 0))
+
     part_b = gram_b.at[pl.ds(0, 16 * (n_ja - 1))]
 
     order_b = jnp.concatenate([slab_b[pl.ds(i, 16, stride=8), :] for i in range(8)], axis=0)
@@ -221,7 +223,7 @@
             p = x * n_ka + k
 
             def hand(x=x, k=k, p=p):
-                send(partial.at[p, pl.ds(0, 1)], partials.at[me, pl.ds(0, 1)], 5, {"ja": x, "ka": k})
+                send(partial.at[p, pl.ds(0, 1)], partials.at[pl.ds(me, 1)], 5, {"ja": x, "ka": k})
 
             if dx or dc:
                 hand()
@@ -231,14 +233,16 @@
 
     @pl.when(z < half)
     def _():
+        share_gram_b()
         lax.fori_loop(0, n_z, functools.partial(weigh, lambda p: inner[p]), 0)
 
     @pl.when(z >= half)
     def _():
         lax.fori_loop(0, n_z, functools.partial(weigh, product), 0)
-
-    partials[me, 0:1, :] = partial[me, 0:1, :]
-    part_r = partials.at[pl.ds(0, n_own - 1), pl.ds(0, 1)]
+        share_gram_b()
+
+    partials[pl.ds(me, 1), :] = partial[me, 0:1, :]
+    part_r = partials.at[pl.ds(0, n_own - 1)]
     sent += [(part_c, 3), (part_b, 4), (part_r, 5)]
 
     wait(part_c, recv_sem.at[3])
@@ -264,7 +268,7 @@
     inverse = jnp.where(lane64 < 64, pltpu.roll(state, 64, 1), state)
 
     wait(part_r, recv_sem.at[5])
-    right = jnp.sum(partials[:, 0, :], axis=0, keepdims=True)
+    right = jnp.sum(partials[...], axis=0, keepdims=True)
     products = inverse * right
     first = jnp.sum(jnp.where(lane64 < 64, products, 0.0), axis=1, keepdims=True)
     second = jnp.sum(jnp.where(lane64 < 64, 0.0, products), axis=1, keepdims=True)
@@ -303,7 +307,7 @@
             pltpu.VMEM((32, 128), F32),
             pltpu.VMEM((n_ja * n_ka, 128, 128), F32),
             pltpu.VMEM((n_ja * n_ka, 8, 128), F32),
-            pltpu.VMEM((n_ja * n_ka, 8, 128), F32),
+            pltpu.VMEM((n_ja * n_ka, 128), F32),
             pltpu.SemaphoreType.DMA((3,)),
             pltpu.SemaphoreType.REGULAR((2,)),
             pltpu.SemaphoreType.DMA((7,)),

time: 31 us -> 30.8 us (level)
  no operation moved by 1% of the time
where the time goes in v4:
time: 30.8 us; the launch traced here: 30.6 us
  Pallas kernels  30.1 us (98%)
  local copies, waits for them, and re-layouts  0.56 us (2%)
    pallas_call x1, Pallas kernels, shards(): pl.pallas_call(functools.partial(kernel, sizes), name='als_update', out_s...  30.1 us

profile of v4, /device:TPU:1, one launch (start us, length us, event | category | flops | bytes accessed | tf_op | source)
XLA Modules:
  0.0 30.6 jit_solution(5649390545272343642)
XLA Ops:
  0.0 30.1 %als_update.1 = f32[1,2,64]{2,1,0:T(2,128)S(1)} custom-call(bf16[128,128,128]{2,1,0:T(8,128)(2,1)} %tensor_ref.1, bf16[1,1,64]{2,1,0:T(2,128)(2,1)} %bitcast.5, bf16[1,4,64]{2,1,0:T(4,128)(2,1)} %bitcast.4), custom_call_target="tpu_custom_call" | custom-call | tf_op jit(solution)/shard_map/als_update/pallas_call | solution.py:288
  30.1 0.6 %copy.5 = f32[64,1,2]{0,2,1:T(2,128)} copy(f32[64,1,2]{0,2,1:T(2,128)S(1)} %bitcast.3) | data formatting | bytes 1024

commit v5 on v4

--- a/solution.py
+++ b/solution.py
@@ -88,6 +88,16 @@
         return 0
 
     lax.fori_loop(2 * z + 2, n_ka, greet_higher, 0)
+
+    def greet_half(k, _):
+        for d in ys:
+            signal(barrier, {"ia": lax.rem(ia + d, n_ia), "ka": k})
+        return 0
+
+    @pl.when(z < half)
+    def _():
+        lax.fori_loop(2 * half, n_ka, greet_half, 0)
+
     load.start()
 
     load_c.wait()
@@ -99,7 +109,8 @@
     piece[4:5, :] = jnp.concatenate([b_row, b_row], axis=1)
     seen[pl.ds(pl.multiple_of(ia * 8, 8), 8), :] = piece[...]
 
-    pl.semaphore_wait(barrier, n_ia + 2 * ja + 2 * z)
+    far = jnp.where(z < half, 0, 2 * half * (n_ia - 1))
+    pl.semaphore_wait(barrier, n_ia + 2 * ja + 2 * z + far)
 
     def greet_lower(k, _):
         signal(ready.at[0], {"ka": k})
@@ -125,6 +136,18 @@
         send(piece, seen.at[pl.ds(pl.multiple_of(ia * 8, 8), 8)], 0, along_y(d))
     lax.fori_loop(0, 2 * z, greet_lower, 0)
     lax.fori_loop(0, ja, greet_lower_x, 0)
+
+    at_own = pl.ds(ka * 8 + ia, 1)
+
+    def send_row(k, _):
+        for d in ys + [0]:
+            send(piece.at[pl.ds(4, 1)], slab_b.at[at_own], 2, {"ia": lax.rem(ia + d, n_ia), "ka": k})
+        return 0
+
+    @pl.when(z >= half)
+    def _():
+        lax.fori_loop(0, 2 * half, send_row, 0)
+
     part = seen.at[pl.ds(0, 8 * (n_ia - 1))]
     sent.append((part, 0))
     wait(part, recv_sem.at[0])
@@ -132,6 +155,14 @@
     @pl.when(ja < n_ja - 1)
     def _():
         pl.semaphore_wait(ready.at[1], 2 * (n_ja - 1 - ja))
+
+    def vouch(k, _):
+        signal(ready.at[2], {"ka": k})
+        return 0
+
+    @pl.when(z >= half)
+    def _():
+        lax.fori_loop(0, 2 * half, vouch, 0)
 
 
     at_b = pl.ds(pl.multiple_of(ka * 8, 8), 8)
@@ -145,7 +176,7 @@
         send(tile_b, slab_b.at[at_b], 2, {"ka": k})
         return 0
 
-    lax.fori_loop(0, 2 * z, send_b, 0)
+    lax.fori_loop(jnp.where(z < half, 0, 2 * half), 2 * z, send_b, 0)
     send_b(2 * z + 1 - core, 0)
 
     @pl.when(z < n_z - 1)
@@ -206,6 +237,10 @@
             send(gram_b.at[at_gram_b], gram_b.at[at_gram_b], 4, along_x(d, 0))
 
     part_b = gram_b.at[pl.ds(0, 16 * (n_ja - 1))]
+
+    @pl.when(z < half)
+    def _():
+        pl.semaphore_wait(ready.at[2], n_ka - 2 * half)
 
     order_b = jnp.concatenate([slab_b[pl.ds(i, 16, stride=8), :] for i in range(8)], axis=0)
     me = ja * n_ka + ka
@@ -233,8 +268,9 @@
 
     @pl.when(z < half)
     def _():
+        weigh(lambda p: inner[p], 0, 0)
         share_gram_b()
-        lax.fori_loop(0, n_z, functools.partial(weigh, lambda p: inner[p]), 0)
+        lax.fori_loop(1, n_z, functools.partial(weigh, lambda p: inner[p]), 0)
 
     @pl.when(z >= half)
     def _():
@@ -309,7 +345,7 @@
             pltpu.VMEM((n_ja * n_ka, 8, 128), F32),
             pltpu.VMEM((n_ja * n_ka, 128), F32),
             pltpu.SemaphoreType.DMA((3,)),
-            pltpu.SemaphoreType.REGULAR((2,)),
+            pltpu.SemaphoreType.REGULAR((3,)),
             pltpu.SemaphoreType.DMA((7,)),
             pltpu.SemaphoreType.DMA((7,)),
         ],

time: 30.8 us -> 30.7 us (level)
  no operation moved by 1% of the time
where the time goes in v5:
time: 30.7 us; the launch traced here: 30.6 us
  Pallas kernels  30 us (98%)
  local copies, waits for them, and re-layouts  0.56 us (2%)
    pallas_call x1, Pallas kernels, shards(): pl.pallas_call(functools.partial(kernel, sizes), name='als_update', out_s...  30 us

profile of v5, /device:TPU:1, one launch (start us, length us, event | category | flops | bytes accessed | tf_op | source)
XLA Modules:
  0.0 30.6 jit_solution(2539190982123371141)
XLA Ops:
  0.0 30.0 %als_update.1 = f32[1,2,64]{2,1,0:T(2,128)S(1)} custom-call(bf16[128,128,128]{2,1,0:T(8,128)(2,1)} %tensor_ref.1, bf16[1,1,64]{2,1,0:T(2,128)(2,1)} %bitcast.5, bf16[1,4,64]{2,1,0:T(4,128)(2,1)} %bitcast.4), custom_call_target="tpu_custom_call" | custom-call | tf_op jit(solution)/shard_map/als_update/pallas_call | solution.py:324
  30.0 0.6 %copy.5 = f32[64,1,2]{0,2,1:T(2,128)} copy(f32[64,1,2]{0,2,1:T(2,128)S(1)} %bitcast.3) | data formatting | bytes 1024
